TPU v7x, 128 devices: a whole 4x4x4 slice. The times are simulated.
128 devices in a mesh: gz: 8 (over y, core), xy: 16 (over z, x).
Axes of the slice: x: 4, y: 4, z: 4, core: 2. Of those that a mesh axis runs over, the one named last changes fastest.
Arguments:
- velocity: float32 [128, 512, 1024], P('gz', 'xy'), may hold values from -6 to 6
- yield_stress: float32 [128, 512, 1024], P('gz', 'xy'), may hold values from 0.2 to 2
- stress_step: float32 [128, 512, 1024], P('gz', 'xy'), may hold values from -6 to 6
- block_weights: bfloat16 [8192, 32, 128], P(('gz', 'xy')), may hold values from -0.5 to 0.5
- block_cells: int32 [8192, 128], P(('gz', 'xy')), may hold values from 0 to 524287
- block_plane: int32 [8192], P(('gz', 'xy')), may hold values from 0 to 40
Outputs:
- stress_product: float32 [128, 512, 1024], P('gz', 'xy')
- plane_obs: float32 [40, 32], replicated
Inputs may be any that keep to these rules, and one draw needn't show every extreme that they name: `block_plane`: value 40 marks an empty slot. `block_cells`: flat index into the brick of the device that holds the block; cells may repeat.
All inputs are finite; a program needn't handle non-finite values.
Results may differ from a plain program's by a relative error of at most 0.0003.
Values sent between devices are 32-bit elements; how exact they have to be, the bound alone decides.
A program may use at most 192 MiB of HBM per device.

v0:
```python
import jax
import jax.numpy as jnp
from jax import lax
from jax.sharding import PartitionSpec as P

PLANES = 40
ITERS = 4


mass_matrix_term = 1.0
viscosity_base = 1.0
damping_factor = 0.8
regular_sq = 0.01


def padded(shard, sides, width):
    for axis, dim in sides:
        size, length = (lax.axis_size(axis), shard.shape[dim])
        up = [(i, (i + 1) % size) for i in range(size - 1)]
        down = [(j, i) for i, j in up]
        last = lax.slice_in_dim(shard, length - width, length, axis=dim)
        initial = lax.slice_in_dim(shard, 0, width, axis=dim)
        before = lax.ppermute(last, axis, up)
        after = lax.ppermute(initial, axis, down)
        shard = jnp.concatenate([before, shard, after], axis=dim)
    return shard


def neighbours(arr):
    centre = arr[1:-1, 1:-1]
    zero = jnp.zeros_like(centre[:, :, :1])
    return (
        centre,
        [
            arr[2:, 1:-1],
            arr[:-2, 1:-1],
            arr[1:-1, 2:],
            arr[1:-1, :-2],
            jnp.concatenate([centre[:, :, 1:], zero], axis=2),
            jnp.concatenate([zero, centre[:, :, :-1]], axis=2),
        ],
    )


def face_flux_sum(coef, field):
    cm, nms = neighbours(coef)
    cv, nvs = neighbours(field)
    total = jnp.zeros_like(cv)
    for nm, nv in zip(nms, nvs):
        total = total + (cm + nm) * 0.5 * (cv - nv)
    return total


def neighbour_weight_sum(coef):
    cm, nms = neighbours(coef)
    total = jnp.full(cm.shape, mass_matrix_term, jnp.float32)
    for nm in nms:
        total = total + (cm + nm) * 0.5
    return total


def cross_sum(first, second):
    cu, nus = neighbours(first)
    cl, nls = neighbours(second)
    total = jnp.zeros_like(cu)
    for nu, nl in zip(nus, nls):
        total = total + (cu - nu) * (cl - nl) * 0.5
    return total


def shear_rate(upad):
    centre = upad[1:-1, 1:-1]
    zero = jnp.zeros_like(centre[:, :, :1])
    dz = upad[2:, 1:-1] - centre
    dy = upad[1:-1, 2:] - centre
    dx = jnp.concatenate([centre[:, :, 1:], zero], axis=2) - centre
    return dz * dz + dy * dy + dx * dx


def shards(velocity, yield_stress, stress_step, block_weights, block_cells, block_plane):
    depth, rows, width = velocity.shape
    upad = padded(velocity, (("gz", 0), ("xy", 1)), 1)
    regul = 1.0 / jnp.sqrt(shear_rate(upad) + regular_sq)
    effective_viscosity = viscosity_base + yield_stress * regul
    dvisc = stress_step * regul
    padded_velocity, padded_derivative = (
        padded(effective_viscosity, (("gz", 0), ("xy", 1)), 1),
        padded(dvisc, (("gz", 0), ("xy", 1)), 1),
    )
    source = -face_flux_sum(padded_derivative, upad)
    diagonal_entries = neighbour_weight_sum(padded_velocity)

    def solve(right_hand_side):
        forward_state = damping_factor * right_hand_side / diagonal_entries
        for sweep in range(ITERS - 1):
            padded_source = padded(forward_state, (("gz", 0), ("xy", 1)), 1)
            forward_state = (
                forward_state
                + damping_factor
                * (
                    right_hand_side
                    - (
                        mass_matrix_term * forward_state
                        + face_flux_sum(padded_velocity, padded_source)
                    )
                )
                / diagonal_entries
            )
        return forward_state

    tangent = solve(source)
    cells = tangent.reshape(-1)[block_cells]
    wts = block_weights.astype(jnp.float32)
    part = jnp.einsum("bsk,bk->bs", wts, cells, precision=lax.Precision.HIGHEST)
    onehot = (block_plane[:, None] == jnp.arange(PLANES, dtype=jnp.int32)[None, :]).astype(
        jnp.float32
    )
    partial_obs = jnp.dot(onehot.T, part, precision=lax.Precision.HIGHEST)
    plane_obs = lax.psum(partial_obs, ("gz", "xy"))
    per_block = jnp.dot(onehot, plane_obs, precision=lax.Precision.HIGHEST)
    back = jnp.einsum("bsk,bs->bk", wts, per_block, precision=lax.Precision.HIGHEST)
    adj_flat = (
        jnp.zeros((depth * rows * width,), jnp.float32)
        .at[block_cells.reshape(-1)]
        .add(back.reshape(-1))
    )
    adj_src = adj_flat.reshape(depth, rows, width)
    adjoint = solve(adj_src)
    apad = padded(adjoint, (("gz", 0), ("xy", 1)), 1)
    product = -regul * cross_sum(upad, apad)
    return (product, plane_obs)


def solution(mesh):
    placed = (
        P("gz", "xy", None),
        P("gz", "xy", None),
        P("gz", "xy", None),
        P(("gz", "xy"), None, None),
        P(("gz", "xy"), None),
        P(("gz", "xy")),
    )
    return jax.shard_map(
        shards, mesh=mesh, in_specs=placed, out_specs=(P("gz", "xy", None), P()), check_vma=False
    )
```

profile of v0, /device:TPU:32, one launch (start us, length us, event | category | flops | bytes accessed | tf_op | source)
XLA Modules:
  0.0 397.8 jit_solution(8668463491863202581)
XLA Ops:
  8.2 4.5 %collective-permute-start.2 = (f32[18,1,1024]{2,0,1:T(8,128)S(1)}, f32[18,1,1024]{2,0,1:T(8,128)S(1)}, u32[]{:S(2)}, u32[]{:S(2)}) collective-permute-start(f32[18,1,1024]{2,0,1:T(8,128)S(1)} %copy.27), channel_id=1, source_target_pairs={{1,0},{2,1},{3,2},{4,3},{5,4},{6,5},{7,6},{8,7},{9,8},{10,9},{11,1... | collective-permute-start | bytes 221192 | tf_op jit(solution)/shard_map/ppermute | solution.py:24
  18.3 5.1 %collective-permute-start.9 = (f32[1,32,1024]{2,1,0:T(8,128)S(1)}, f32[1,32,1024]{2,1,0:T(8,128)S(1)}, u32[]{:S(2)}, u32[]{:S(2)}) collective-permute-start(f32[1,32,1024]{2,1,0:T(8,128)S(1)} %get-tuple-element.66), channel_id=1, source_target_pairs={{0,16},{16,32},{32,48},{48,64},{64,80},{80,96},{96,112},{1,17},{17... | collective-permute-start | bytes 393224 | tf_op jit(solution)/shard_map/ppermute | solution.py:23
  24.8 4.3 %collective-permute-start.4 = (f32[1,32,1024]{2,1,0:T(8,128)S(1)}, f32[1,32,1024]{2,1,0:T(8,128)S(1)}, u32[]{:S(2)}, u32[]{:S(2)}) collective-permute-start(f32[1,32,1024]{2,1,0:T(8,128)S(1)} %get-tuple-element.60), channel_id=1, source_target_pairs={{0,16},{16,32},{32,48},{48,64},{64,80},{80,96},{96,112},{1,17},{17... | collective-permute-start | bytes 393224 | tf_op jit(solution)/shard_map/ppermute | solution.py:23
  32.6 4.7 %collective-permute-start.10 = (f32[18,1,1024]{2,0,1:T(8,128)S(1)}, f32[18,1,1024]{2,0,1:T(8,128)S(1)}, u32[]{:S(2)}, u32[]{:S(2)}) collective-permute-start(f32[18,1,1024]{2,0,1:T(8,128)S(1)} %copy.35), channel_id=1, source_target_pairs={{1,0},{2,1},{3,2},{4,3},{5,4},{6,5},{7,6},{8,7},{9,8},{10,9},{11,1... | collective-permute-start | bytes 221192 | tf_op jit(solution)/shard_map/ppermute | solution.py:24
  39.5 6.0 %collective-permute-start.5 = (f32[18,1,1024]{2,0,1:T(8,128)S(1)}, f32[18,1,1024]{2,0,1:T(8,128)S(1)}, u32[]{:S(2)}, u32[]{:S(2)}) collective-permute-start(f32[18,1,1024]{2,0,1:T(8,128)S(1)} %copy.29), channel_id=1, source_target_pairs={{1,0},{2,1},{3,2},{4,3},{5,4},{6,5},{7,6},{8,7},{9,8},{10,9},{11,1... | collective-permute-start | bytes 221192 | tf_op jit(solution)/shard_map/ppermute | solution.py:24
  47.5 4.5 %fusion.185 = (f32[16,32,1023]{2,1,0:T(8,128)}, f32[16,32,1023]{2,1,0:T(8,128)}, f32[16,32,1023]{2,1,0:T(8,128)}, f32[16,32,1023]{2,1,0:T(8,128)}) fusion(f32[16,32,1024]{2,1,0:T(8,128)S(1)} %get-tuple-element.9, f32[16,32,1024]{2,1,0:T(8,128)S(1)} %get-tuple-element.8), kind=kLoop, calls=%fused_computation.304 | loop fusion | bytes 16760832 | tf_op jit(solution)/shard_map/slice | solution.py:40
  55.3 9.0 %fusion.158 = (f32[16,32,1024]{2,1,0:T(8,128)S(1)}, f32[16,32,1024]{2,1,0:T(8,128)S(1)}, f32[16,32,1024]{2,1,0:T(8,128)S(1)}, f32[16,32,1024]{2,1,0:T(8,128)S(1)}) fusion(f32[16,32,1024]{2,1,0:T(8,128)S(1)} %get-tuple-element.9, f32[1,32,1024]{2,1,0:T(8,128)S(1)} %collective-permute-done.8, f32[1,32,1024]{2,1,0:T(8,128)S(1)} %collective-permute-done.9, ...), kind=kLoop, calls=%fused_computation.239 | loop fusion | flops 36700160 | bytes 30838784 | tf_op jit(solution)/shard_map/div | solution.py:94
  76.8 5.3 %collective-permute-done.15 = f32[18,1,1024]{2,0,1:T(8,128)S(1)} collective-permute-done((f32[18,1,1024]{2,0,1:T(8,128)S(1)}, f32[18,1,1024]{2,0,1:T(8,128)S(1)}, u32[]{:S(2)}, u32[]{:S(2)}) %collective-permute-start.15) | collective-permute-done | bytes 73760 | tf_op jit(solution)/shard_map/ppermute | solution.py:23
  82.2 5.0 %fusion.114 = f32[16,32,1024]{2,1,0:T(8,128)S(1)} fusion(f32[16,32,1024]{2,1,0:T(8,128)S(1)} %get-tuple-element.4, f32[16,32,1024]{2,1,0:T(8,128)S(1)} %get-tuple-element.5, f32[18,1,1024]{2,1,0:T(1,128)S(1)} %copy.42, f32[1,32,1024]{2,1,0:T(8,128)S(1)} %collective-permute-done.12, f32[1,32,1024]{2,1,0:T(8,128)S(1)} %collective-permute-done.13, ...), kind=kLoop, calls=%fused_computation.165 | loop fusion | flops 27262976 | bytes 17592320 | tf_op jit(solution)/shard_map/add | solution.py:98
  104.1 5.0 %fusion.96 = f32[16,32,1024]{2,1,0:T(8,128)S(1)} fusion(f32[16,32,1024]{2,1,0:T(8,128)S(1)} %fusion.114, f32[16,32,1024]{2,1,0:T(8,128)S(1)} %get-tuple-element.5, f32[18,1,1024]{2,1,0:T(1,128)S(1)} %copy.46, f32[1,32,1024]{2,1,0:T(8,128)S(1)} %collective-permute-done.16, f32[1,32,1024]{2,1,0:T(8,128)S(1)} %collective-permute-done.17, ...), kind=kLoop, calls=%fused_computation.139 | loop fusion | flops 27262976 | bytes 17592320 | tf_op jit(solution)/shard_map/add | solution.py:98
  110.4 6.2 %collective-permute-start.21 = (f32[1,32,1024]{2,1,0:T(8,128)S(1)}, f32[1,32,1024]{2,1,0:T(8,128)S(1)}, u32[]{:S(2)}, u32[]{:S(2)}) collective-permute-start(f32[1,32,1024]{2,1,0:T(8,128)S(1)} %get-tuple-element.48), channel_id=1, source_target_pairs={{0,16},{16,32},{32,48},{48,64},{64,80},{80,96},{96,112},{1,17},{17... | collective-permute-start | bytes 393224 | tf_op jit(solution)/shard_map/ppermute | solution.py:23
  128.4 5.0 %fusion.78 = f32[16,32,1024]{2,1,0:T(8,128)S(1)} fusion(f32[16,32,1024]{2,1,0:T(8,128)S(1)} %fusion.96, f32[16,32,1024]{2,1,0:T(8,128)S(1)} %get-tuple-element.5, f32[18,1,1024]{2,1,0:T(1,128)S(1)} %copy.50, f32[1,32,1024]{2,1,0:T(8,128)S(1)} %collective-permute-done.20, f32[1,32,1024]{2,1,0:T(8,128)S(1)} %collective-permute-done.21, ...), kind=kLoop, calls=%fused_computation.113 | loop fusion | flops 27262976 | bytes 17592320 | tf_op jit(solution)/shard_map/add | solution.py:98
  133.9 45.5 %gather_fusion = f32[8192]{0:T(1024)S(1)} fusion(f32[524288]{0:T(1024)S(1)} %bitcast.27, s32[8192]{0:T(1024)S(1)} %fusion.163), kind=kCustom, calls=%fused_computation | custom fusion | bytes 98304 | tf_op jit(solution)/shard_map/gather | solution.py:112
  180.6 69.8 %psum.7 = f32[40,32]{0,1:T(8,128)S(1)} all-reduce(f32[40,32]{0,1:T(8,128)S(1)} %fusion.165), channel_id=1, replica_groups=mesh['gz'=8,'xy'=16] {'gz','xy'}, use_global_device_ids=true, to_apply=%region_0.0 | all-reduce | flops 1280 | bytes 10240 | tf_op jit(solution)/shard_map/psum | solution.py:119
  251.1 44.6 %scatter_custom_fusion = f32[524288]{0:T(1024)} fusion(s32[8192]{0:T(1024)S(1)} %bitcast.30, f32[8192]{0:T(1024)S(1)} %bitcast.32, f32[]{:T(128)} %constant.7.clone.1), kind=kCustom, calls=%fused_computation.247 | custom fusion | flops 8192 | bytes 2097156 | tf_op jit(solution)/shard_map/scatter-add | solution.py:125
  298.6 4.4 %multiply_divide_fusion = f32[16,32,1024]{2,1,0:T(8,128)S(1)} fusion(f32[16,32,1024]{2,1,0:T(8,128)} %reshape.48, f32[16,32,1024]{2,1,0:T(8,128)} %copy-done.5, f32[16,32,1024]{2,1,0:T(8,128)} %copy-done.3, f32[16,32,1024]{2,1,0:T(8,128)S(1)} %copy-done.2, f32[1,32,1024]{2,1,0:T(8,128)S(1)} %copy-done.17, f32[1,32,1024]{2,1,0:T(8,128)S(1)} %copy-done.19, ...), kind=kLoop, calls=%fused_computation.236 | loop fusion | flops 12582912 | bytes 10895360 | tf_op jit(solution)/shard_map/div | solution.py:94
  308.5 4.3 %collective-permute-start.26 = (f32[18,1,1024]{2,0,1:T(8,128)S(1)}, f32[18,1,1024]{2,0,1:T(8,128)S(1)}, u32[]{:S(2)}, u32[]{:S(2)}) collective-permute-start(f32[18,1,1024]{2,0,1:T(8,128)S(1)} %copy.51), channel_id=1, source_target_pairs={{1,0},{2,1},{3,2},{4,3},{5,4},{6,5},{7,6},{8,7},{9,8},{10,9},{11,1... | collective-permute-start | bytes 221192 | tf_op jit(solution)/shard_map/ppermute | solution.py:24
  316.4 5.4 %collective-permute-done.27 = f32[18,1,1024]{2,0,1:T(8,128)S(1)} collective-permute-done((f32[18,1,1024]{2,0,1:T(8,128)S(1)}, f32[18,1,1024]{2,0,1:T(8,128)S(1)}, u32[]{:S(2)}, u32[]{:S(2)}) %collective-permute-start.27) | collective-permute-done | bytes 73760 | tf_op jit(solution)/shard_map/ppermute | solution.py:23
  321.9 4.9 %fusion.60 = f32[16,32,1024]{2,1,0:T(8,128)S(1)} fusion(f32[16,32,1024]{2,1,0:T(8,128)S(1)} %multiply_divide_fusion, f32[16,32,1024]{2,1,0:T(8,128)S(1)} %copy-done.9, f32[18,1,1024]{2,1,0:T(1,128)S(1)} %copy.54, f32[1,32,1024]{2,1,0:T(8,128)S(1)} %collective-permute-done.24, f32[1,32,1024]{2,1,0:T(8,128)S(1)} %collective-permute-done.25, ...), kind=kLoop, calls=%fused_computation.87 | loop fusion | flops 27262976 | bytes 17592320 | tf_op jit(solution)/shard_map/add | solution.py:98
  343.4 4.9 %fusion.42 = f32[16,32,1024]{2,1,0:T(8,128)S(1)} fusion(f32[16,32,1024]{2,1,0:T(8,128)S(1)} %fusion.60, f32[16,32,1024]{2,1,0:T(8,128)S(1)} %copy-done.9, f32[18,1,1024]{2,1,0:T(1,128)S(1)} %copy.58, f32[1,32,1024]{2,1,0:T(8,128)S(1)} %collective-permute-done.28, f32[1,32,1024]{2,1,0:T(8,128)S(1)} %collective-permute-done.29, f32[18,1,1024]{2,1,0:T(1,128)S(1)} %copy.56, ...), kind=kLoop, calls=%fused_computation.61 | loop fusion | flops 27262976 | bytes 17592320 | tf_op jit(solution)/shard_map/add | solution.py:98
  349.6 6.2 %collective-permute-start.33 = (f32[1,32,1024]{2,1,0:T(8,128)S(1)}, f32[1,32,1024]{2,1,0:T(8,128)S(1)}, u32[]{:S(2)}, u32[]{:S(2)}) collective-permute-start(f32[1,32,1024]{2,1,0:T(8,128)S(1)} %get-tuple-element.36), channel_id=1, source_target_pairs={{0,16},{16,32},{32,48},{48,64},{64,80},{80,96},{96,112},{1,17},{17... | collective-permute-start | bytes 393224 | tf_op jit(solution)/shard_map/ppermute | solution.py:23
  367.6 4.9 %fusion.24 = f32[16,32,1024]{2,1,0:T(8,128)S(1)} fusion(f32[16,32,1024]{2,1,0:T(8,128)S(1)} %fusion.42, f32[16,32,1024]{2,1,0:T(8,128)S(1)} %copy-done.9, f32[18,1,1024]{2,1,0:T(1,128)S(1)} %copy.62, f32[1,32,1024]{2,1,0:T(8,128)S(1)} %collective-permute-done.32, f32[1,32,1024]{2,1,0:T(8,128)S(1)} %collective-permute-done.33, f32[18,1,1024]{2,1,0:T(1,128)S(1)} %copy.60, ...), kind=kLoop, calls=%fused_computation.35 | loop fusion | flops 27262976 | bytes 17592320 | tf_op jit(solution)/shard_map/add | solution.py:98
  373.8 5.9 %collective-permute-start.37 = (f32[1,32,1024]{2,1,0:T(8,128)S(1)}, f32[1,32,1024]{2,1,0:T(8,128)S(1)}, u32[]{:S(2)}, u32[]{:S(2)}) collective-permute-start(f32[1,32,1024]{2,1,0:T(8,128)S(1)} %get-tuple-element.32), channel_id=1, source_target_pairs={{0,16},{16,32},{32,48},{48,64},{64,80},{80,96},{96,112},{1,17},{17... | collective-permute-start | bytes 393224 | tf_op jit(solution)/shard_map/ppermute | solution.py:23
  391.9 5.8 %fusion.6 = f32[16,32,1024]{2,1,0:T(8,128)} fusion(f32[16,32,1024]{2,1,0:T(8,128)S(1)} %fusion.24, f32[18,1,1024]{2,1,0:T(1,128)S(1)} %copy.66, f32[1,32,1024]{2,1,0:T(8,128)S(1)} %collective-permute-done.36, f32[1,32,1024]{2,1,0:T(8,128)S(1)} %collective-permute-done.37, f32[18,1,1024]{2,1,0:T(1,128)S(1)} %copy.64, ...), kind=kLoop, calls=%fused_computation.9 | loop fusion | flops 24641536 | bytes 17850368 | tf_op jit(solution)/shard_map/mul | solution.py:130
  (227 shorter events, 124.2 us)
Async XLA Ops:
  17.0 15.4 %collective-permute-start.8 = (f32[1,32,1024]{2,1,0:T(8,128)S(1)}, f32[1,32,1024]{2,1,0:T(8,128)S(1)}, u32[]{:S(2)}, u32[]{:S(2)}) collective-permute-start(f32[1,32,1024]{2,1,0:T(8,128)S(1)} %get-tuple-element.67), channel_id=1, source_target_pairs={{16,0},{32,16},{48,32},{64,48},{80,64},{96,80},{112,96},{17,1},{33... | collective-permute-start | bytes 393224 | tf_op jit(solution)/shard_map/ppermute | solution.py:24
  18.3 14.1 %collective-permute-start.9 = (f32[1,32,1024]{2,1,0:T(8,128)S(1)}, f32[1,32,1024]{2,1,0:T(8,128)S(1)}, u32[]{:S(2)}, u32[]{:S(2)}) collective-permute-start(f32[1,32,1024]{2,1,0:T(8,128)S(1)} %get-tuple-element.66), channel_id=1, source_target_pairs={{0,16},{16,32},{32,48},{48,64},{64,80},{80,96},{96,112},{1,17},{17... | collective-permute-start | bytes 393224 | tf_op jit(solution)/shard_map/ppermute | solution.py:23
  23.5 15.8 %collective-permute-start.3 = (f32[1,32,1024]{2,1,0:T(8,128)S(1)}, f32[1,32,1024]{2,1,0:T(8,128)S(1)}, u32[]{:S(2)}, u32[]{:S(2)}) collective-permute-start(f32[1,32,1024]{2,1,0:T(8,128)S(1)} %get-tuple-element.61), channel_id=1, source_target_pairs={{16,0},{32,16},{48,32},{64,48},{80,64},{96,80},{112,96},{17,1},{33... | collective-permute-start | bytes 393224 | tf_op jit(solution)/shard_map/ppermute | solution.py:24
  24.8 14.5 %collective-permute-start.4 = (f32[1,32,1024]{2,1,0:T(8,128)S(1)}, f32[1,32,1024]{2,1,0:T(8,128)S(1)}, u32[]{:S(2)}, u32[]{:S(2)}) collective-permute-start(f32[1,32,1024]{2,1,0:T(8,128)S(1)} %get-tuple-element.60), channel_id=1, source_target_pairs={{0,16},{16,32},{32,48},{48,64},{64,80},{80,96},{96,112},{1,17},{17... | collective-permute-start | bytes 393224 | tf_op jit(solution)/shard_map/ppermute | solution.py:23
  29.1 22.9 %collective-permute-start.7 = (f32[18,1,1024]{2,0,1:T(8,128)S(1)}, f32[18,1,1024]{2,0,1:T(8,128)S(1)}, u32[]{:S(2)}, u32[]{:S(2)}) collective-permute-start(f32[18,1,1024]{2,0,1:T(8,128)S(1)} %copy.33), channel_id=1, source_target_pairs={{0,1},{1,2},{2,3},{3,4},{4,5},{5,6},{6,7},{7,8},{8,9},{9,10},{10,1... | collective-permute-start | bytes 221192 | tf_op jit(solution)/shard_map/ppermute | solution.py:23
  32.6 19.5 %collective-permute-start.10 = (f32[18,1,1024]{2,0,1:T(8,128)S(1)}, f32[18,1,1024]{2,0,1:T(8,128)S(1)}, u32[]{:S(2)}, u32[]{:S(2)}) collective-permute-start(f32[18,1,1024]{2,0,1:T(8,128)S(1)} %copy.35), channel_id=1, source_target_pairs={{1,0},{2,1},{3,2},{4,3},{5,4},{6,5},{7,6},{8,7},{9,8},{10,9},{11,1... | collective-permute-start | bytes 221192 | tf_op jit(solution)/shard_map/ppermute | solution.py:24
  37.4 14.9 %collective-permute-start.11 = (f32[18,1,1024]{2,0,1:T(8,128)S(1)}, f32[18,1,1024]{2,0,1:T(8,128)S(1)}, u32[]{:S(2)}, u32[]{:S(2)}) collective-permute-start(f32[18,1,1024]{2,0,1:T(8,128)S(1)} %copy.37), channel_id=1, source_target_pairs={{0,1},{1,2},{2,3},{3,4},{4,5},{5,6},{6,7},{7,8},{8,9},{9,10},{10,1... | collective-permute-start | bytes 221192 | tf_op jit(solution)/shard_map/ppermute | solution.py:23
  39.5 12.9 %collective-permute-start.5 = (f32[18,1,1024]{2,0,1:T(8,128)S(1)}, f32[18,1,1024]{2,0,1:T(8,128)S(1)}, u32[]{:S(2)}, u32[]{:S(2)}) collective-permute-start(f32[18,1,1024]{2,0,1:T(8,128)S(1)} %copy.29), channel_id=1, source_target_pairs={{1,0},{2,1},{3,2},{4,3},{5,4},{6,5},{7,6},{8,7},{9,8},{10,9},{11,1... | collective-permute-start | bytes 221192 | tf_op jit(solution)/shard_map/ppermute | solution.py:24
  45.6 9.6 %collective-permute-start.6 = (f32[18,1,1024]{2,0,1:T(8,128)S(1)}, f32[18,1,1024]{2,0,1:T(8,128)S(1)}, u32[]{:S(2)}, u32[]{:S(2)}) collective-permute-start(f32[18,1,1024]{2,0,1:T(8,128)S(1)} %copy.31), channel_id=1, source_target_pairs={{0,1},{1,2},{2,3},{3,4},{4,5},{5,6},{6,7},{7,8},{8,9},{9,10},{10,1... | collective-permute-start | bytes 221192 | tf_op jit(solution)/shard_map/ppermute | solution.py:23
  73.4 8.8 %collective-permute-start.15 = (f32[18,1,1024]{2,0,1:T(8,128)S(1)}, f32[18,1,1024]{2,0,1:T(8,128)S(1)}, u32[]{:S(2)}, u32[]{:S(2)}) collective-permute-start(f32[18,1,1024]{2,0,1:T(8,128)S(1)} %copy.41), channel_id=1, source_target_pairs={{0,1},{1,2},{2,3},{3,4},{4,5},{5,6},{6,7},{7,8},{8,9},{9,10},{10,1... | collective-permute-start | bytes 221192 | tf_op jit(solution)/shard_map/ppermute | solution.py:23
  95.4 8.6 %collective-permute-start.19 = (f32[18,1,1024]{2,0,1:T(8,128)S(1)}, f32[18,1,1024]{2,0,1:T(8,128)S(1)}, u32[]{:S(2)}, u32[]{:S(2)}) collective-permute-start(f32[18,1,1024]{2,0,1:T(8,128)S(1)} %copy.45), channel_id=1, source_target_pairs={{0,1},{1,2},{2,3},{3,4},{4,5},{5,6},{6,7},{7,8},{8,9},{9,10},{10,1... | collective-permute-start | bytes 221192 | tf_op jit(solution)/shard_map/ppermute | solution.py:23
  109.1 7.6 %collective-permute-start.20 = (f32[1,32,1024]{2,1,0:T(8,128)S(1)}, f32[1,32,1024]{2,1,0:T(8,128)S(1)}, u32[]{:S(2)}, u32[]{:S(2)}) collective-permute-start(f32[1,32,1024]{2,1,0:T(8,128)S(1)} %get-tuple-element.49), channel_id=1, source_target_pairs={{16,0},{32,16},{48,32},{64,48},{80,64},{96,80},{112,96},{17,1},{33... | collective-permute-start | bytes 393224 | tf_op jit(solution)/shard_map/ppermute | solution.py:24
  110.4 7.2 %collective-permute-start.21 = (f32[1,32,1024]{2,1,0:T(8,128)S(1)}, f32[1,32,1024]{2,1,0:T(8,128)S(1)}, u32[]{:S(2)}, u32[]{:S(2)}) collective-permute-start(f32[1,32,1024]{2,1,0:T(8,128)S(1)} %get-tuple-element.48), channel_id=1, source_target_pairs={{0,16},{16,32},{32,48},{48,64},{64,80},{80,96},{96,112},{1,17},{17... | collective-permute-start | bytes 393224 | tf_op jit(solution)/shard_map/ppermute | solution.py:23
  119.7 8.6 %collective-permute-start.23 = (f32[18,1,1024]{2,0,1:T(8,128)S(1)}, f32[18,1,1024]{2,0,1:T(8,128)S(1)}, u32[]{:S(2)}, u32[]{:S(2)}) collective-permute-start(f32[18,1,1024]{2,0,1:T(8,128)S(1)} %copy.49), channel_id=1, source_target_pairs={{0,1},{1,2},{2,3},{3,4},{4,5},{5,6},{6,7},{7,8},{8,9},{9,10},{10,1... | collective-permute-start | bytes 221192 | tf_op jit(solution)/shard_map/ppermute | solution.py:23
  308.5 7.8 %collective-permute-start.26 = (f32[18,1,1024]{2,0,1:T(8,128)S(1)}, f32[18,1,1024]{2,0,1:T(8,128)S(1)}, u32[]{:S(2)}, u32[]{:S(2)}) collective-permute-start(f32[18,1,1024]{2,0,1:T(8,128)S(1)} %copy.51), channel_id=1, source_target_pairs={{1,0},{2,1},{3,2},{4,3},{5,4},{6,5},{7,6},{8,7},{9,8},{10,9},{11,1... | collective-permute-start | bytes 221192 | tf_op jit(solution)/shard_map/ppermute | solution.py:24
  312.9 8.9 %collective-permute-start.27 = (f32[18,1,1024]{2,0,1:T(8,128)S(1)}, f32[18,1,1024]{2,0,1:T(8,128)S(1)}, u32[]{:S(2)}, u32[]{:S(2)}) collective-permute-start(f32[18,1,1024]{2,0,1:T(8,128)S(1)} %copy.53), channel_id=1, source_target_pairs={{0,1},{1,2},{2,3},{3,4},{4,5},{5,6},{6,7},{7,8},{8,9},{9,10},{10,1... | collective-permute-start | bytes 221192 | tf_op jit(solution)/shard_map/ppermute | solution.py:23
  334.7 8.6 %collective-permute-start.31 = (f32[18,1,1024]{2,0,1:T(8,128)S(1)}, f32[18,1,1024]{2,0,1:T(8,128)S(1)}, u32[]{:S(2)}, u32[]{:S(2)}) collective-permute-start(f32[18,1,1024]{2,0,1:T(8,128)S(1)} %copy.57), channel_id=1, source_target_pairs={{0,1},{1,2},{2,3},{3,4},{4,5},{5,6},{6,7},{7,8},{8,9},{9,10},{10,1... | collective-permute-start | bytes 221192 | tf_op jit(solution)/shard_map/ppermute | solution.py:23
  348.3 7.5 %collective-permute-start.32 = (f32[1,32,1024]{2,1,0:T(8,128)S(1)}, f32[1,32,1024]{2,1,0:T(8,128)S(1)}, u32[]{:S(2)}, u32[]{:S(2)}) collective-permute-start(f32[1,32,1024]{2,1,0:T(8,128)S(1)} %get-tuple-element.37), channel_id=1, source_target_pairs={{16,0},{32,16},{48,32},{64,48},{80,64},{96,80},{112,96},{17,1},{33... | collective-permute-start | bytes 393224 | tf_op jit(solution)/shard_map/ppermute | solution.py:24
  349.6 7.2 %collective-permute-start.33 = (f32[1,32,1024]{2,1,0:T(8,128)S(1)}, f32[1,32,1024]{2,1,0:T(8,128)S(1)}, u32[]{:S(2)}, u32[]{:S(2)}) collective-permute-start(f32[1,32,1024]{2,1,0:T(8,128)S(1)} %get-tuple-element.36), channel_id=1, source_target_pairs={{0,16},{16,32},{32,48},{48,64},{64,80},{80,96},{96,112},{1,17},{17... | collective-permute-start | bytes 393224 | tf_op jit(solution)/shard_map/ppermute | solution.py:23
  358.9 8.6 %collective-permute-start.35 = (f32[18,1,1024]{2,0,1:T(8,128)S(1)}, f32[18,1,1024]{2,0,1:T(8,128)S(1)}, u32[]{:S(2)}, u32[]{:S(2)}) collective-permute-start(f32[18,1,1024]{2,0,1:T(8,128)S(1)} %copy.61), channel_id=1, source_target_pairs={{0,1},{1,2},{2,3},{3,4},{4,5},{5,6},{6,7},{7,8},{8,9},{9,10},{10,1... | collective-permute-start | bytes 221192 | tf_op jit(solution)/shard_map/ppermute | solution.py:23
  372.5 7.3 %collective-permute-start.36 = (f32[1,32,1024]{2,1,0:T(8,128)S(1)}, f32[1,32,1024]{2,1,0:T(8,128)S(1)}, u32[]{:S(2)}, u32[]{:S(2)}) collective-permute-start(f32[1,32,1024]{2,1,0:T(8,128)S(1)} %get-tuple-element.33), channel_id=1, source_target_pairs={{16,0},{32,16},{48,32},{64,48},{80,64},{96,80},{112,96},{17,1},{33... | collective-permute-start | bytes 393224 | tf_op jit(solution)/shard_map/ppermute | solution.py:24
  373.8 6.9 %collective-permute-start.37 = (f32[1,32,1024]{2,1,0:T(8,128)S(1)}, f32[1,32,1024]{2,1,0:T(8,128)S(1)}, u32[]{:S(2)}, u32[]{:S(2)}) collective-permute-start(f32[1,32,1024]{2,1,0:T(8,128)S(1)} %get-tuple-element.32), channel_id=1, source_target_pairs={{0,16},{16,32},{32,48},{48,64},{64,80},{80,96},{96,112},{1,17},{17... | collective-permute-start | bytes 393224 | tf_op jit(solution)/shard_map/ppermute | solution.py:23
  380.9 7.1 %collective-permute-start.38 = (f32[18,1,1024]{2,0,1:T(8,128)S(1)}, f32[18,1,1024]{2,0,1:T(8,128)S(1)}, u32[]{:S(2)}, u32[]{:S(2)}) collective-permute-start(f32[18,1,1024]{2,0,1:T(8,128)S(1)} %copy.63), channel_id=1, source_target_pairs={{1,0},{2,1},{3,2},{4,3},{5,4},{6,5},{7,6},{8,7},{9,8},{10,9},{11,1... | collective-permute-start | bytes 221192 | tf_op jit(solution)/shard_map/ppermute | solution.py:24
  382.9 8.9 %collective-permute-start.39 = (f32[18,1,1024]{2,0,1:T(8,128)S(1)}, f32[18,1,1024]{2,0,1:T(8,128)S(1)}, u32[]{:S(2)}, u32[]{:S(2)}) collective-permute-start(f32[18,1,1024]{2,0,1:T(8,128)S(1)} %copy.65), channel_id=1, source_target_pairs={{0,1},{1,2},{2,3},{3,4},{4,5},{5,6},{6,7},{7,8},{8,9},{9,10},{10,1... | collective-permute-start | bytes 221192 | tf_op jit(solution)/shard_map/ppermute | solution.py:23
  (55 other events, 1147.0 us)
where the time goes:
time: 404 us; the launch traced here: 398 us
  starting transfers between devices  121 us (30%)
  other arithmetic  96.3 us (24%)
  blocking collectives  69.8 us (17%)
  local copies, waits for them, and re-layouts  65.4 us (16%)
  waiting for transfers between devices  41.4 us (10%)
    ppermute x20, starting transfers between devices, padded(): before = lax.ppermute(last, axis, up)  75.2 us
    psum x1, blocking collectives, shards(): plane_obs = lax.psum(partial_obs, ('gz', 'xy'))  69.8 us
    ppermute x20, starting transfers between devices, padded(): after = lax.ppermute(initial, axis, down)  45.5 us
    gather x1, local copies, waits for them, and re-layouts, shards(): cells = tangent.reshape(-1)[block_cells]  45.5 us
    scatter-add x1, other arithmetic, shards(): adj_flat = jnp.zeros((depth * rows * width,), jnp.float32).at[block_cells...  44.6 us
    ppermute x20, waiting for transfers between devices, padded(): before = lax.ppermute(last, axis, up)  38.6 us
    add x6, other arithmetic, solve(): forward_state + damping_factor * (right_hand_side - (mass_matrix_term * f...  29.5 us
    div x2, other arithmetic, solve(): forward_state = damping_factor * right_hand_side / diagonal_entries  13.4 us
  transfers between devices with their start and end apart: 40, of which 17 were waited for; matrix products, arithmetic and copies ran while one was open for 4% of the time, Pallas kernels for 0%

commit v1 on v0

v1 whole, which is shorter than its diff:
```python
import functools
import jax
import jax.numpy as jnp
from jax import lax
from jax.experimental import pallas as pl
from jax.experimental.pallas import tpu as pltpu
from jax.sharding import PartitionSpec as P

PLANES = 40
KEEP = 0.2
DAMP = 0.8
MESH = pl.DeviceIdType.MESH
F32 = jnp.float32
BF16 = jnp.bfloat16
VMEM = pl.BlockSpec(memory_space=pltpu.VMEM)
SMEM = pl.BlockSpec(memory_space=pltpu.SMEM)
ANY = pl.BlockSpec(memory_space=pl.ANY)
LIMIT = 56 * 1024 * 1024


def ids(shape):
    rank = len(shape)
    return (
        lax.broadcasted_iota(jnp.int32, shape, rank - 2),
        lax.broadcasted_iota(jnp.int32, shape, rank - 1),
    )


def x_next(a, wrap=True):
    sub, lane = ids(a.shape)
    r = pltpu.roll(a, 127, a.ndim - 1)
    r = jnp.where(lane == 127, pltpu.roll(r, 7, a.ndim - 2), r)
    return r if wrap else jnp.where((lane == 127) & (sub == 7), 0.0, r)


def x_prev(a, wrap=True):
    sub, lane = ids(a.shape)
    r = pltpu.roll(a, 1, a.ndim - 1)
    r = jnp.where(lane == 0, pltpu.roll(r, 1, a.ndim - 2), r)
    return r if wrap else jnp.where((lane == 0) & (sub == 0), 0.0, r)


def divisor(n, most):
    return max(d for d in range(1, most + 1) if n % d == 0)


class Faces:
    def __init__(self, CZ, CY, send, recv):
        self.CZ, self.CY, self.send, self.recv = CZ, CY, send, recv
        G, X = lax.axis_size("gz"), lax.axis_size("xy")
        g, x = lax.axis_index("gz"), lax.axis_index("xy")
        self.has = (g > 0, g < G - 1, x > 0, x < X - 1)
        lower, upper = jnp.maximum(g - 1, 0), jnp.minimum(g + 1, G - 1)
        left, right = jnp.maximum(x - 1, 0), jnp.minimum(x + 1, X - 1)
        self.to = ((lower, x), (upper, x), (g, left), (g, right))

    def barrier(self):
        sem = pltpu.get_barrier_semaphore()
        count = jnp.int32(0)
        for has, to in zip(self.has, self.to):
            count = count + has.astype(jnp.int32)

            @pl.when(has)
            def _():
                pl.semaphore_signal(sem, inc=1, device_id=to, device_id_type=MESH)

        pl.semaphore_wait(sem, count)

    def copy(self, buf, e, d):
        CZ, CY = self.CZ, self.CY
        zs, ys = pl.ds(1, CZ), pl.ds(1, CY)
        src = (buf.at[1, ys], buf.at[CZ, ys], buf.at[zs, 1], buf.at[zs, CY])[d]
        dst = (buf.at[CZ + 1, ys], buf.at[0, ys], buf.at[zs, CY + 1], buf.at[zs, 0])[d]
        return pltpu.make_async_remote_copy(
            src_ref=src,
            dst_ref=dst,
            send_sem=self.send.at[e, d],
            recv_sem=self.recv.at[e, d],
            device_id=self.to[d],
            device_id_type=MESH,
        )

    def start(self, buf, e):
        for d in range(4):

            @pl.when(self.has[d])
            def _():
                self.copy(buf, e, d).start()

    def arrive(self, buf, e):
        for d in range(4):

            @pl.when(self.has[d ^ 1])
            def _():
                self.copy(buf, e, d).wait_recv()

    def finish(self, buf, e):
        for d in range(4):

            @pl.when(self.has[d])
            def _():
                self.copy(buf, e, d).wait_send()


def clear_faces(bufs, CZ, CY):
    plane = jnp.zeros((CY + 2, 8, 128), F32)
    row = jnp.zeros((CZ, 8, 128), F32)
    for buf in bufs:
        buf[0] = plane
        buf[CZ + 1] = plane
        buf[pl.ds(1, CZ), 0] = row
        buf[pl.ds(1, CZ), CY + 1] = row


def interior(CZ, CY, f):
    yn = divisor(CY - 2, 10)
    per = (CY - 2) // yn

    @pl.loop(0, (CZ - 2) * per)
    def _(i):
        f(1 + i // per, 1 + (i % per) * yn, 1, yn)


def boundary(CZ, CY, f):
    yn = divisor(CY, 8)
    per = CY // yn
    zn = divisor(CZ - 2, 8)
    parts = (CZ - 2) // zn

    @pl.loop(0, 2 * per)
    def _(i):
        f((i // per) * (CZ - 1), (i % per) * yn, 1, yn)

    @pl.loop(0, 2 * parts)
    def _(i):
        f(1 + (i % parts) * zn, (i // parts) * (CY - 1), zn, 1)


def around(ref, z, y, zn, yn):
    zs, ys = pl.ds(z + 1, zn), pl.ds(y + 1, yn)
    if zn == 1:
        wide = ref[zs, pl.ds(y, yn + 2)]
        return (
            wide[:, 1 : yn + 1],
            wide[:, :yn],
            wide[:, 2:],
            ref[pl.ds(z, 1), ys],
            ref[pl.ds(z + 2, 1), ys],
        )
    wide = ref[pl.ds(z, zn + 2), ys]
    return (
        wide[1 : zn + 1],
        ref[zs, pl.ds(y, yn)],
        ref[zs, pl.ds(y + 2, yn)],
        wide[:zn],
        wide[2:],
    )


def coefficients(MU, z, y, zn, yn):
    m, ym, yp, zm, zp = around(MU, z, y, zn, yn)
    xm, xp = x_prev(m, False), x_next(m, False)
    total = ((xm + xp) + (ym + yp)) + (zm + zp)
    dinv = DAMP / (1.0 + (3.0 * m + 0.5 * total))
    half = 0.5 * dinv
    sub, lane = ids(m.shape)
    first, last = (sub == 0) & (lane == 0), (sub == 7) & (lane == 127)
    faces = (
        jnp.where(first, 0.0, half * (m + xm)),
        jnp.where(last, 0.0, half * (m + xp)),
        half * (m + ym),
        half * (m + yp),
        half * (m + zm),
        half * (m + zp),
    )
    return faces, dinv


def sweep(A, R, src, dst, pad, z, y, zn, yn):
    w, ym, yp, zm, zp = around(src, z, y, zn, yn)
    zs, ys = pl.ds(z, zn), pl.ds(y, yn)
    total = KEEP * w + R[zs, ys]
    for at, value in enumerate((x_prev(w), x_next(w), ym, yp, zm, zp)):
        total = total + A[at, zs, ys] * value
    dst[pl.ds(z + pad, zn), pl.ds(y + pad, yn)] = total


def tangent_kernel(
    CZ, CY, v_in, y_in, s_in, tan_out, mu_out, v_out, reg_out,
    vin, yin, sin, V, MU, DMU, REG, A, R, W1, W2, W3, T, load, store, send, recv,
):
    tiles = CY // 8
    loads = [
        pltpu.make_async_copy(src, dst, load.at[i])
        for i, (src, dst) in enumerate(((v_in, vin), (y_in, yin), (s_in, sin)))
    ]
    for c in loads:
        c.start()
    faces = Faces(CZ, CY, send, recv)
    clear_faces((V, MU, DMU, W1, W2, W3), CZ, CY)
    faces.barrier()
    loads[0].wait()

    @pl.loop(0, CZ * tiles)
    def _(i):
        z, y = i // tiles, (i % tiles) * 8
        for s in range(8):
            V[z + 1, y + 1 + s] = vin[i, pl.ds(s, 8, stride=8), :]

    faces.start(V, 0)
    loads[1].wait()
    loads[2].wait()

    def viscosity(z, t):
        i, y = z * tiles + t, t * 8
        here = pl.ds(y + 1, 8)
        c = V[z + 1, here]
        dz = V[z + 2, here] - c
        dy = V[z + 1, pl.ds(y + 2, 8)] - c
        dx = x_next(c, False) - c
        reg = lax.rsqrt((dz * dz + dy * dy + dx * dx) + 0.01)
        REG[z, pl.ds(y, 8)] = reg
        for s in range(8):
            MU[z + 1, y + 1 + s] = 1.0 + yin[i, pl.ds(s, 8, stride=8), :] * reg[s]
            DMU[z + 1, y + 1 + s] = sin[i, pl.ds(s, 8, stride=8), :] * reg[s]

    @pl.loop(0, (CZ - 1) * (tiles - 1))
    def _(i):
        viscosity(i // (tiles - 1), i % (tiles - 1))

    faces.arrive(V, 0)

    @pl.loop(0, CZ)
    def _(i):
        viscosity(i, tiles - 1)

    @pl.loop(0, tiles - 1)
    def _(i):
        viscosity(CZ - 1, i)

    faces.start(MU, 1)
    faces.start(DMU, 2)

    def source(z, y, zn, yn):
        zs, ys = pl.ds(z, zn), pl.ds(y, yn)
        face, dinv = coefficients(MU, z, y, zn, yn)
        for at in range(6):
            A[at, zs, ys] = face[at]
        d, *ds = around(DMU, z, y, zn, yn)
        v, *vs = around(V, z, y, zn, yn)
        ds += [x_prev(d, False), x_next(d, False)]
        vs += [x_prev(v, False), x_next(v, False)]
        total = (d + ds[0]) * (vs[0] - v)
        for dn, vn in zip(ds[1:], vs[1:]):
            total = total + (d + dn) * (vn - v)
        first = (0.5 * dinv) * total
        R[zs, ys] = first
        W1[pl.ds(z + 1, zn), pl.ds(y + 1, yn)] = first

    interior(CZ, CY, source)
    faces.arrive(MU, 1)
    faces.arrive(DMU, 2)
    stores = [
        pltpu.make_async_copy(src, dst, store.at[i])
        for i, (src, dst) in enumerate(((MU, mu_out), (V, v_out), (REG, reg_out)))
    ]
    for c in stores:
        c.start()
    boundary(CZ, CY, source)
    for step, (src, dst, pad) in enumerate(((W1, W2, 1), (W2, W3, 1), (W3, T, 0))):
        faces.start(src, 3 + step)
        go = functools.partial(sweep, A, R, src, dst, pad)
        interior(CZ, CY, go)
        faces.arrive(src, 3 + step)
        boundary(CZ, CY, go)
    last = pltpu.make_async_copy(T, tan_out, store.at[3])
    last.start()
    for e, buf in enumerate((V, MU, DMU, W1, W2, W3)):
        faces.finish(buf, e)
    for c in stores + [last]:
        c.wait()


def adjoint_kernel(
    CZ, CY, q_in, mu_in, v_in, reg_in, out,
    Q, MU, V, REG, A, R, W1, W2, W3, W4, T, load, store, send, recv,
):
    loads = [
        pltpu.make_async_copy(src, dst, load.at[i])
        for i, (src, dst) in enumerate(((mu_in, MU), (q_in, Q), (v_in, V), (reg_in, REG)))
    ]
    for c in loads:
        c.start()
    faces = Faces(CZ, CY, send, recv)
    clear_faces((W1, W2, W3, W4), CZ, CY)
    faces.barrier()
    loads[0].wait()
    loads[1].wait()

    def begin(z, y, zn, yn):
        zs, ys = pl.ds(z, zn), pl.ds(y, yn)
        face, dinv = coefficients(MU, z, y, zn, yn)
        for at in range(6):
            A[at, zs, ys] = face[at]
        first = dinv * Q[zs, ys]
        R[zs, ys] = first
        W1[pl.ds(z + 1, zn), pl.ds(y + 1, yn)] = first

    def product(z, y, zn, yn):
        zs, ys = pl.ds(z, zn), pl.ds(y, yn)
        v, *vs = around(V, z, y, zn, yn)
        a, *many = around(W4, z, y, zn, yn)
        vs += [x_prev(v, False), x_next(v, False)]
        many += [x_prev(a, False), x_next(a, False)]
        total = (v - vs[0]) * (a - many[0])
        for vn, an in zip(vs[1:], many[1:]):
            total = total + (v - vn) * (a - an)
        T[zs, ys] = (-0.5 * REG[zs, ys]) * total

    boundary(CZ, CY, begin)
    faces.start(W1, 0)
    interior(CZ, CY, begin)
    for step, (src, dst) in enumerate(((W1, W2), (W2, W3), (W3, W4))):
        if step:
            faces.start(src, step)
        go = functools.partial(sweep, A, R, src, dst, 1)
        interior(CZ, CY, go)
        faces.arrive(src, step)
        boundary(CZ, CY, go)
    faces.start(W4, 3)
    loads[2].wait()
    loads[3].wait()
    interior(CZ, CY, product)
    faces.arrive(W4, 3)
    boundary(CZ, CY, product)
    last = pltpu.make_async_copy(T, out, store)
    last.start()
    for e, buf in enumerate((W1, W2, W3, W4)):
        faces.finish(buf, e)
    last.wait()


def gather_kernel(B, K, cells_s, plane_s, cells_v, weights, field, out, rows):
    @pl.loop(0, B)
    def _(b):
        for k in range(K):
            r = cells_s[b, k] >> 7
            rows[b, pl.ds(k, 1), :] = field[pl.ds(r, 1), :]

    step = divisor(B, 8)
    sub, _ = ids((128, K))
    _, lane = ids((8, 128))

    def group(g, acc):
        low, high = acc
        inner = cells_v[g] & 127
        for j in range(step):
            b = g * step + j
            hot = jnp.where(sub == inner[j : j + 1, :], 1.0, 0.0).T
            picked = rows[b] * hot
            main = picked.astype(BF16)
            rest = (picked - main.astype(F32)).astype(BF16)
            w = weights[b]
            part = jnp.dot(w, main, preferred_element_type=F32) + jnp.dot(
                w, rest, preferred_element_type=F32
            )
            total = jnp.sum(part, axis=1, keepdims=True)
            p = plane_s[b]
            p = jnp.where(p < PLANES, p, -1000)
            for n in range(3):
                low = low + jnp.where(lane == p + PLANES * n, total[8 * n : 8 * n + 8], 0.0)
            high = high + jnp.where(lane == p, total[24:32], 0.0)
        return low, high

    zero = jnp.zeros((8, 128), F32)
    low, high = lax.fori_loop(0, B // step, group, (zero, zero))
    out[0:8, :] = low
    out[8:16, :] = high


def sum_kernel(G, X, part, out, one, two, mid, s1, r1, s2, r2):
    g, x = lax.axis_index("gz"), lax.axis_index("xy")
    sem = pltpu.get_barrier_semaphore()
    for d in range(1, G):
        pl.semaphore_signal(sem, inc=1, device_id=(lax.rem(g + d, G), x), device_id_type=MESH)
    for d in range(1, X):
        pl.semaphore_signal(sem, inc=1, device_id=(g, lax.rem(x + d, X)), device_id_type=MESH)
    pl.semaphore_wait(sem, G + X - 2)

    def stage(src, buf, me, n, target, send, recv):
        copies = []
        for d in range(1, n):
            c = pltpu.make_async_remote_copy(
                src_ref=src,
                dst_ref=buf.at[me],
                send_sem=send.at[d],
                recv_sem=recv.at[d],
                device_id=target(lax.rem(me + d, n)),
                device_id_type=MESH,
            )
            c.start()
            copies.append(c)
        buf[me] = src[...]
        for c in copies:
            c.wait_recv()
        total = buf[0]
        for i in range(1, n):
            total = total + buf[i]
        return total, copies

    total, first = stage(part, one, g, G, lambda t: (t, x), s1, r1)
    mid[...] = total
    total, second = stage(mid, two, x, X, lambda t: (g, t), s2, r2)
    out[...] = total
    for c in first + second:
        c.wait_send()


def scatter_kernel(B, K, copies, cells_s, plane_s, cells_v, weights, table, out, obs, values, *accs):
    rows = out.shape[0]

    @pl.loop(0, rows // 64)
    def _(i):
        for acc in accs:
            acc[pl.ds(i * 64, 64), :] = jnp.zeros((64, 128), F32)

    step = divisor(B, 8)
    sub, _ = ids((128, K))
    _, lane = ids((32, 128))
    packed = table[...]
    low = packed[0:8]
    po = jnp.concatenate(
        [low, pltpu.roll(low, 128 - PLANES, 1), pltpu.roll(low, 128 - 2 * PLANES, 1), packed[8:16]],
        axis=0,
    )
    po = jnp.where(lane < PLANES, po, 0.0)
    obs[...] = po[:, :PLANES]

    @pl.loop(0, B // step)
    def _(g):
        inner = cells_v[g] & 127
        for j in range(step):
            b = g * step + j
            mine = jnp.sum(jnp.where(lane == plane_s[b], po, 0.0), axis=1, keepdims=True)
            back = jnp.sum(weights[b].astype(F32) * mine, axis=0, keepdims=True)
            values[b] = jnp.where(sub == inner[j : j + 1, :], back, 0.0).T

    @pl.loop(0, B)
    def _(b):
        for k in range(0, K, copies):
            at = [pl.ds(cells_s[b, k + j] >> 7, 1) for j in range(copies)]
            new = [accs[j][at[j], :] + values[b, pl.ds(k + j, 1), :] for j in range(copies)]
            for j in range(copies):
                accs[j][at[j], :] = new[j]

    @pl.loop(0, rows // 64)
    def _(i):
        here = pl.ds(i * 64, 64)
        total = accs[0][here, :]
        for acc in accs[1:]:
            total = total + acc[here, :]
        out[here, :] = total


def shards(velocity, yield_stress, stress_step, block_weights, block_cells, block_plane):
    CZ, CY, NX = velocity.shape
    B, S, K = block_weights.shape
    G, X = lax.axis_size("gz"), lax.axis_size("xy")
    core, padded = (CZ, CY, 8, 128), (CZ + 2, CY + 2, 8, 128)
    tiles = (CZ * CY // 8, 64, 128)

    def tiled(field):
        return field.reshape(CZ, CY // 8, 8, 8, 128).transpose(0, 1, 3, 2, 4).reshape(tiles)

    def sds(shape):
        return jax.ShapeDtypeStruct(shape, F32)

    def vm(shape):
        return pltpu.VMEM(shape, F32)

    def params(n=None):
        if n is None:
            return pltpu.CompilerParams(vmem_limit_bytes=LIMIT)
        return pltpu.CompilerParams(vmem_limit_bytes=LIMIT, collective_id=n, has_side_effects=True)

    DMA = pltpu.SemaphoreType.DMA
    tangent, mu, vel, reg = pl.pallas_call(
        functools.partial(tangent_kernel, CZ, CY),
        out_shape=(sds(core), sds(padded), sds(padded), sds(core)),
        in_specs=[ANY] * 3,
        out_specs=(ANY,) * 4,
        scratch_shapes=[vm(tiles)] * 3 + [vm(padded)] * 3 + [vm(core), vm((6,) + core), vm(core)]
        + [vm(padded)] * 3 + [vm(core), DMA((3,)), DMA((4,)), DMA((6, 4)), DMA((6, 4))],
        compiler_params=params(0),
        name="tangent",
    )(tiled(velocity), tiled(yield_stress), tiled(stress_step))

    groups = divisor(B, 8)
    cells_v = block_cells.reshape(B // groups, groups, K)
    part = pl.pallas_call(
        functools.partial(gather_kernel, B, K),
        out_shape=sds((16, 128)),
        in_specs=[SMEM, SMEM, VMEM, VMEM, VMEM],
        out_specs=VMEM,
        scratch_shapes=[vm((B, K, 128))],
        compiler_params=params(),
        name="gather",
    )(block_cells, block_plane, cells_v, block_weights, tangent.reshape(CZ * CY * 8, 128))

    table = pl.pallas_call(
        functools.partial(sum_kernel, G, X),
        out_shape=sds((16, 128)),
        in_specs=[VMEM],
        out_specs=VMEM,
        scratch_shapes=[vm((G, 16, 128)), vm((X, 16, 128)), vm((16, 128)), DMA((G,)), DMA((G,)), DMA((X,)), DMA((X,))],
        compiler_params=params(1),
        name="sum",
    )(part)

    copies = 8
    adj, obs = pl.pallas_call(
        functools.partial(scatter_kernel, B, K, copies),
        out_shape=(sds((CZ * CY * 8, 128)), sds((S, PLANES))),
        in_specs=[SMEM, SMEM, VMEM, VMEM, VMEM],
        out_specs=(VMEM, VMEM),
        scratch_shapes=[vm((B, K, 128))] + [vm((CZ * CY * 8, 128))] * copies,
        compiler_params=params(),
        name="scatter",
    )(block_cells, block_plane, cells_v, block_weights, table)

    product = pl.pallas_call(
        functools.partial(adjoint_kernel, CZ, CY),
        out_shape=sds(core),
        in_specs=[ANY] * 4,
        out_specs=ANY,
        scratch_shapes=[vm(core), vm(padded), vm(padded), vm(core), vm((6,) + core), vm(core)]
        + [vm(padded)] * 4 + [vm(core), DMA((4,)), DMA, DMA((4, 4)), DMA((4, 4))],
        compiler_params=params(2),
        name="adjoint",
    )(adj.reshape(core), mu, vel, reg)
    return product.reshape(CZ, CY, NX), obs.T


def solution(mesh):
    placed = (
        P("gz", "xy", None),
        P("gz", "xy", None),
        P("gz", "xy", None),
        P(("gz", "xy"), None, None),
        P(("gz", "xy"), None),
        P(("gz", "xy")),
    )
    return jax.shard_map(
        shards, mesh=mesh, in_specs=placed, out_specs=(P("gz", "xy", None), P()), check_vma=False
    )
```

time: 404 us -> 125 us (0.31); the launches traced: 398 us -> 124 us
  Pallas kernels: 0 us -> 121 us
  starting transfers between devices: 121 us -> 0 us
  other arithmetic: 96.3 us -> 0 us
  blocking collectives: 69.8 us -> 0 us
  local copies, waits for them, and re-layouts: 65.4 us -> 2.7 us
  waiting for transfers between devices: 41.4 us -> 0 us
    ppermute x40 -> x0, starting transfers between devices: 121 us -> none  [the longest x20 75.2 us: padded(): before = lax.ppermute(last, axis, up)]
    pallas_call x0 -> x5, Pallas kernels: none -> 121 us  [the longest x1 36.7 us: shards(): pl.pallas_call(functools.partial(tangent_kernel, CZ, CY), out_shape=(sds(...]
    psum x1 -> x0, blocking collectives: 69.8 us -> none  [shards(): plane_obs = lax.psum(partial_obs, ('gz', 'xy'))]
    gather x1 -> x0, local copies, waits for them, and re-layouts: 45.5 us -> none  [shards(): cells = tangent.reshape(-1)[block_cells]]
    scatter-add x1 -> x0, other arithmetic: 44.6 us -> none  [shards(): adj_flat = jnp.zeros((depth * rows * width,), jnp.float32).at[block_cells...]
    ppermute x40 -> x0, waiting for transfers between devices: 41.4 us -> none  [the longest x20 38.6 us: padded(): before = lax.ppermute(last, axis, up)]
    add x6 -> x0, other arithmetic: 29.5 us -> none  [solve(): forward_state + damping_factor * (right_hand_side - (mass_matrix_term * f...]
    div x2 -> x0, other arithmetic: 13.4 us -> none  [solve(): forward_state = damping_factor * right_hand_side / diagonal_entries]
  transfers between devices with their start and end apart: 40 -> 0, of which waited for: 17 -> 0; matrix products, arithmetic and copies ran while one was open for 4% -> 0% of each run, Pallas kernels for 0% -> 0%
where the time goes in v1:
time: 125 us; the launch traced here: 124 us
  Pallas kernels  121 us (97%)
  local copies, waits for them, and re-layouts  2.7 us (2%)
    pallas_call x1, Pallas kernels, shards(): pl.pallas_call(functools.partial(tangent_kernel, CZ, CY), out_shape=(sds(...  36.7 us
    pallas_call x1, Pallas kernels, shards(): pl.pallas_call(functools.partial(adjoint_kernel, CZ, CY), out_shape=sds(c...  35.7 us
    pallas_call x1, Pallas kernels, shards(): pl.pallas_call(functools.partial(scatter_kernel, B, K, copies), out_shape...  16.6 us
    pallas_call x1, Pallas kernels, shards(): pl.pallas_call(functools.partial(gather_kernel, B, K), out_shape=sds((16,...  16.1 us
    pallas_call x1, Pallas kernels, shards(): pl.pallas_call(functools.partial(sum_kernel, G, X), out_shape=sds((16, 12...  15.5 us
    reshape x1, local copies, waits for them, and re-layouts, shards(): return (product.reshape(CZ, CY, NX), obs.T)  2.7 us

profile of v1, /device:TPU:32, one launch (start us, length us, event | category | flops | bytes accessed | tf_op | source)
XLA Modules:
  0.0 124.0 jit_solution(10946879625590980865)
XLA Ops:
  0.6 36.7 %tangent.1 = (f32[16,32,8,128]{3,2,1,0:T(8,128)}, f32[18,34,8,128]{3,2,1,0:T(8,128)}, f32[18,34,8,128]{3,2,1,0:T(8,128)}, f32[16,32,8,128]{3,2,1,0:T(8,128)}) custom-call(f32[64,64,128]{2,1,0:T(8,128)} %bitcast.21, f32[64,64,128]{2,1,0:T(8,128)} %bitcast.22, f32[64,64,128]{2,1,0:T(8,128)} %bitcast.23), custom_call_target="tpu_custom_call" | custom-call | tf_op jit(solution)/shard_map/tangent/pallas_call | solution.py:487
  37.4 16.1 %gather.1.part = f32[16,128]{1,0:T(8,128)} custom-call(s32[64,128]{1,0:T(8,128)} %cells_s.3, s32[64]{0:T(128)} %plane_s.3, s32[8,8,128]{2,1,0:T(8,128)} %bitcast.26, bf16[64,32,128]{2,1,0:T(8,128)(2,1)} %weights.3, f32[4096,128]{1,0:T(8,128)} %bitcast.24), custom_call_target="tpu_custom_call" | custom-call | tf_op jit(solution)/shard_map/gather/pallas_call | solution.py:500
  53.5 15.5 %sum.1.table = f32[16,128]{1,0:T(8,128)} custom-call(f32[16,128]{1,0:T(8,128)} %gather.1.part), custom_call_target="tpu_custom_call" | custom-call | tf_op jit(solution)/shard_map/sum/pallas_call | solution.py:510
  69.0 16.6 %scatter.1 = (f32[4096,128]{1,0:T(8,128)}, f32[32,40]{1,0:T(8,128)}) custom-call(s32[64,128]{1,0:T(8,128)} %cells_s.3, s32[64]{0:T(128)} %plane_s.3, s32[8,8,128]{2,1,0:T(8,128)} %bitcast.27, bf16[64,32,128]{2,1,0:T(8,128)(2,1)} %weights.3, f32[16,128]{1,0:T(8,128)} %sum.1.table), custom_call_target="tpu_custom_call" | custom-call | tf_op jit(solution)/shard_map/scatter/pallas_call | solution.py:521
  85.6 35.7 %adjoint.1 = f32[16,32,8,128]{3,2,1,0:T(8,128)} custom-call(f32[16,32,8,128]{3,2,1,0:T(8,128)} %bitcast.25, f32[18,34,8,128]{3,2,1,0:T(8,128)} %get-tuple-element.10.mu_in, f32[18,34,8,128]{3,2,1,0:T(8,128)} %get-tuple-element.11.v_in, f32[16,32,8,128]{3,2,1,0:T(8,128)} %get-tuple-element.12.reg_in), custom_call_target="tpu_custom_call" | custom-call | tf_op jit(solution)/shard_map/adjoint/pallas_call | solution.py:531
  121.3 2.7 %reshape.43 = f32[16,32,1024]{2,1,0:T(8,128)} reshape(f32[16,32,8,128]{3,2,1,0:T(8,128)} %adjoint.1) | data formatting | bytes 4194304 | tf_op jit(solution)/shard_map/reshape | solution.py:541
